TPU v7x, 32 devices: a whole 2x2x4 slice. The times are simulated.
32 devices in a mesh: px: 8 (over y, x, core), py: 4 (over z).
Axes of the slice: x: 2, y: 2, z: 4, core: 2. Of those that a mesh axis runs over, the one named last changes fastest.
Arguments:
- base_flow: float32 [768, 384, 768], P('px', 'py'), may hold values from -6 to 6
- tangent: float32 [768, 384, 768], P('px', 'py'), may hold values from -6 to 6
- kx_bounds: int32 [2, 320], replicated, may hold values from 0 to 320, as said below
- left_basis: float32 [384, 384], replicated, may hold values from -0.3125 to 0.3125
- right_basis: float32 [384, 384], replicated, may hold values from -0.3125 to 0.3125
- eigenvalues: float32 [384], replicated, may hold values from 0.05 to 20
- wall_rows: float32 [2, 384], replicated, may hold values from -0.3125 to 0.3125
- sources: float32 [2, 384], replicated, may hold values from -6 to 6
- influence: float32 [4, 320, 320], P(None, 'py', 'px'), may hold values from -6 to 6
Outputs:
- response: float32 [384, 320, 2, 320], P(None, 'py', None, 'px')
Inputs may be any that keep to these rules, and one draw needn't show every extreme that they name: kx_bounds[0, b] is at most 80 and kx_bounds[1, b] at least 240; the first column keeps every streamwise wavenumber.
All inputs are finite; a program needn't handle non-finite values.
Results may differ from a plain program's by a relative error of at most 0.000078.
Values sent between devices are 32-bit elements; how exact they have to be, the bound alone decides.
A program may use at most 192 MiB of HBM per device.

v0:
```python
import math

import jax
import jax.numpy as jnp
from jax import lax
from jax.sharding import PartitionSpec as P

NX = 768
NY = 384
NZ = 768
MX = 160
MZ = 160
KX = 320
KZ = 320


def dft_tables(length, kept, half):
    points = jnp.arange(length, dtype=jnp.int32)
    waves = jnp.arange(kept, dtype=jnp.int32) - half
    turns = waves[:, None] * points[None, :] % length
    angles = turns.astype(jnp.float32) * (2.0 * math.pi / length)
    scale_factor = 1.0 / math.sqrt(length)
    return (jnp.cos(angles) * scale_factor, jnp.sin(angles) * scale_factor)


def body(
    base_flow,
    tangent,
    kx_bounds,
    left_basis,
    right_basis,
    eigenvalues,
    wall_rows,
    sources,
    influence,
):
    highest = lax.Precision.HIGHEST
    product = base_flow * tangent
    x_count = product.shape[0]
    y_count = product.shape[1]
    z_cosine, z_sine = dft_tables(NZ, KZ, MZ)
    z_table = jnp.concatenate([z_cosine, -z_sine], axis=0)
    z_modes = jnp.einsum(
        "xyn,kn->yxk", product, z_table, precision=highest, preferred_element_type=jnp.float32
    )
    z_modes = z_modes.reshape(y_count, x_count, 2, KZ)
    x_cosine, x_sine = dft_tables(NX, KX, MX)
    x_table = jnp.concatenate([x_cosine, x_sine], axis=0)
    block = lax.all_to_all(z_modes, "px", split_axis=3, concat_axis=1, tiled=True)
    items = block.shape[0]
    kz_count = block.shape[3]
    flat = block.reshape(items, NX, 2 * kz_count)
    mixed = jnp.einsum(
        "kn,ynq->ykq", x_table, flat, precision=highest, preferred_element_type=jnp.float32
    )
    mixed = mixed.reshape(items, 2, KX, 2, kz_count)
    real_part = mixed[:, 0, :, 0] + mixed[:, 1, :, 1]
    imag_part = mixed[:, 0, :, 1] - mixed[:, 1, :, 0]
    modes = jnp.stack([real_part, imag_part], axis=2)
    kz_local = modes.shape[3]
    kz_start = lax.axis_index("px") * kz_local
    kx_scaled = (jnp.arange(KX) - MX).astype(jnp.float32) / MX
    factor = kx_scaled[None, :, None]
    bounds_here = lax.dynamic_slice_in_dim(kx_bounds, kz_start, kz_local, 1)
    columns = jnp.arange(KX, dtype=jnp.int32)
    keep_mask = (columns[:, None] >= bounds_here[0][None, :]) & (
        columns[:, None] < bounds_here[1][None, :]
    )
    keep_mask = keep_mask[None, :, :]
    forcing_real = jnp.where(keep_mask, -factor * modes[:, :, 1, :], 0.0)
    forcing_imag = jnp.where(keep_mask, factor * modes[:, :, 0, :], 0.0)
    forcing = jnp.stack([forcing_real, forcing_imag], axis=2)
    forcing = lax.all_to_all(forcing, "py", split_axis=1, concat_axis=0, tiled=True)
    kx_local = forcing.shape[1]
    kx_start = lax.axis_index("py") * kx_local
    kx_here = (kx_start + jnp.arange(kx_local, dtype=jnp.int32) - MX).astype(jnp.float32) / MX
    kz_here = (kz_start + jnp.arange(kz_local, dtype=jnp.int32) - MZ).astype(jnp.float32) / MZ
    shift = kx_here[:, None] ** 2 + kz_here[None, :] ** 2
    mode_gain = 1.0 / (1.0 + eigenvalues[:, None, None, None] + shift[None, :, None, :])
    full_shape = forcing.shape
    projected = jnp.dot(
        left_basis, forcing.reshape(NY, -1), precision=highest, preferred_element_type=jnp.float32
    )
    weighted = mode_gain * projected.reshape(full_shape)
    source_proj = jnp.dot(
        left_basis, jnp.transpose(sources), precision=highest, preferred_element_type=jnp.float32
    )
    source_weighted = mode_gain * source_proj[:, None, :, None]
    inverse_map = influence.reshape(2, 2, kx_local, kz_local)
    particular = jnp.dot(
        right_basis, weighted.reshape(NY, -1), precision=highest, preferred_element_type=jnp.float32
    )
    homogeneous = jnp.dot(
        right_basis,
        source_weighted.reshape(NY, -1),
        precision=highest,
        preferred_element_type=jnp.float32,
    )
    wall_values = jnp.dot(
        wall_rows, particular, precision=highest, preferred_element_type=jnp.float32
    )
    particular = particular.reshape(full_shape)
    homogeneous = homogeneous.reshape(full_shape)
    solve_wall_values = wall_values.reshape((2,) + full_shape[1:])
    first_coef = -(
        inverse_map[0, 0][:, None, :] * solve_wall_values[0]
        + inverse_map[0, 1][:, None, :] * solve_wall_values[1]
    )
    second_coef = -(
        inverse_map[1, 0][:, None, :] * solve_wall_values[0]
        + inverse_map[1, 1][:, None, :] * solve_wall_values[1]
    )
    first_coef, second_coef = (first_coef, second_coef)
    response = (
        particular
        + first_coef[None] * homogeneous[:, :, 0:1, :]
        + second_coef[None] * homogeneous[:, :, 1:2, :]
    )
    return response


def solution(mesh):
    placed = (
        P("px", "py", None),
        P("px", "py", None),
        P(),
        P(),
        P(),
        P(),
        P(),
        P(),
        P(None, "py", "px"),
    )
    return jax.shard_map(
        body, mesh=mesh, in_specs=placed, out_specs=P(None, "py", None, "px"), check_vma=False
    )
```

profile of v0, /device:TPU:11, one launch (start us, length us, event | category | flops | bytes accessed | tf_op | source)
XLA Modules:
  0.0 1158.1 jit_solution(13004709458691551400)
XLA Ops:
  0.0 4.1 sine_multiply_fusion
  4.1 73.2 %fusion.2 = f32[96,96,640]{2,0,1:T(8,128)} fusion(f32[96,96,768]{2,1,0:T(8,128)} %param.9, f32[96,96,768]{2,1,0:T(8,128)} %param.10, f32[320,768]{1,0:T(8,128)S(1)} %get-tuple-element.22, f32[320,768]{1,0:T(8,128)S(1)} %get-tuple-element.23), kind=kOutput, calls=%fused_computation.8 | convolution fusion | flops 54365749248 | bytes 82182144 | tf_op jit(solution)/shard_map/xyn,kn->yxk/dot_general | solution.py:43
  77.4 33.0 %reshape.224 = f32[96,96,2,320]{3,2,0,1:T(2,128)} reshape(f32[96,96,640]{2,0,1:T(8,128)} %fusion.2) | data formatting | bytes 47185920 | tf_op jit(solution)/shard_map/reshape | solution.py:46
  110.3 63.0 %copy.29 = f32[96,96,2,320]{1,2,0,3:T(2,128)} copy(f32[96,96,2,320]{3,2,0,1:T(2,128)} %reshape.224) | data formatting | bytes 47185920 | tf_op jit(solution)/shard_map/reshape | solution.py:46
  173.4 8.1 all-to-all-start
  181.5 0.8 constant_dynamic-slice_fusion
  182.4 338.9 %all-to-all-done = f32[96,96,2,320]{1,2,0,3:T(2,128)} async-done(((f32[96,96,2,320]{1,2,0,3:T(2,128)}), f32[96,96,2,320]{1,2,0,3:T(2,128)}, u32[]{:S(2)}, u32[]{:S(2)}) %all-to-all-start) | async-done | bytes 23592992 | tf_op jit(solution)/shard_map/all_to_all | solution.py:49
  521.2 16.6 %copy.30 = f32[96,96,2,320]{1,3,2,0:T(8,128)S(1)} copy(f32[96,96,2,320]{1,2,0,3:T(2,128)} %all-to-all-done) | data formatting | bytes 47185920 | tf_op jit(solution)/shard_map/all_to_all | solution.py:49
  537.9 11.8 %copy.31 = f32[96,8,96,2,40]{2,1,4,3,0:T(8,128)} copy(f32[96,8,96,2,40]{2,4,1,3,0:T(8,128)S(1)} %bitcast.84) | data formatting | bytes 47185920 | tf_op jit(solution)/shard_map/all_to_all | solution.py:49
  549.7 31.2 %reshape.225 = f32[96,768,80]{1,2,0:T(8,128)} reshape(f32[96,8,96,2,40]{2,1,4,3,0:T(8,128)} %copy.31) | data formatting | bytes 47185920 | tf_op jit(solution)/shard_map/reshape | solution.py:52
  580.9 61.4 %convolution_bitcast_fusion.1 = f32[96,640,80]{1,2,0:T(8,128)} fusion(f32[96,768,80]{1,2,0:T(8,128)} %reshape.225, f32[320,768]{1,0:T(8,128)S(1)} %get-tuple-element.22, f32[320,768]{1,0:T(8,128)S(1)} %get-tuple-element.21), kind=kOutput, calls=%fused_computation.7 | convolution fusion | flops 45298974720 | bytes 45219840 | tf_op jit(solution)/shard_map/kn,ynq->ykq/dot_general | solution.py:53
  642.3 27.7 %reshape.226 = f32[96,2,320,2,40]{2,1,4,3,0:T(2,128)} reshape(f32[96,640,80]{1,2,0:T(8,128)} %convolution_bitcast_fusion.1) | data formatting | bytes 39321600 | tf_op jit(solution)/shard_map/reshape | solution.py:56
  670.0 30.9 %fusion.23 = (f32[96,1,320,1,40]{2,1,4,3,0:T(1,128)}, f32[96,1,320,1,40]{2,1,4,3,0:T(1,128)}, f32[96,1,320,1,40]{2,1,4,3,0:T(1,128)}, f32[96,1,320,1,40]{2,1,4,3,0:T(1,128)}) fusion(f32[96,2,320,2,40]{2,1,4,3,0:T(2,128)} %reshape.226), kind=kLoop, calls=%fused_computation.52 | loop fusion | bytes 39321600 | tf_op jit(solution)/shard_map/slice | solution.py:58
  700.9 12.0 %copy.41 = f32[96,1,320,1,40]{0,4,2,3,1:T(8,128)} copy(f32[96,1,320,1,40]{2,1,4,3,0:T(1,128)} %get-tuple-element.9) | data formatting | bytes 9830400
  712.8 12.0 %copy.42 = f32[96,1,320,1,40]{0,4,2,3,1:T(8,128)} copy(f32[96,1,320,1,40]{2,1,4,3,0:T(1,128)} %get-tuple-element.7) | data formatting | bytes 9830400
  724.9 12.0 %copy.43 = f32[96,1,320,1,40]{0,4,2,3,1:T(8,128)} copy(f32[96,1,320,1,40]{2,1,4,3,0:T(1,128)} %get-tuple-element.8) | data formatting | bytes 9830400
  736.9 12.2 %copy.44 = f32[96,1,320,1,40]{0,4,2,3,1:T(8,128)} copy(f32[96,1,320,1,40]{2,1,4,3,0:T(1,128)} %get-tuple-element.10) | data formatting | bytes 9830400
  749.0 16.3 %fusion.6 = (f32[96,320,1,40]{0,3,2,1:T(8,128)}, f32[96,320,1,40]{0,3,2,1:T(8,128)}) fusion(f32[96,1,320,1,40]{0,4,2,3,1:T(8,128)} %copy.41, f32[96,1,320,1,40]{0,4,2,3,1:T(8,128)} %copy.42, f32[320]{0:T(512)S(1)} %get-tuple-element.27, pred[320,40]{1,0:T(8,128)(4,1)S(1)} %fusion.19, f32[96,1,320,1,40]{0,4,2,3,1:T(8,128)} %copy.43, ...), kind=kLoop, calls=%fused_computation.13 | loop fusion | flops 7372800 | bytes 29506560 | tf_op jit(solution)/shard_map/jit(_where)/select_n | solution.py:70
  765.3 10.3 pad_maximum_fusion
  775.6 6.5 all-to-all-start.1
  783.3 0.8 add_divide_fusion
  784.0 4.9 bitcast_multiply_fusion
  788.9 23.8 %fusion.27 = f32[6400,384]{1,0:T(8,128)S(1)} fusion(f32[384,6400]{0,1:T(8,128)} %bitcast_multiply_fusion, f32[384,384]{1,0:T(8,128)S(1)} %copy-done), kind=kOutput, calls=%fused_computation.56 | convolution fusion | flops 11324620800 | bytes 20250624 | tf_op jit(solution)/shard_map/dot_general | solution.py:93
  812.8 4.4 slice_bitcast_fusion.1
  817.2 246.1 %all-to-all-done.1 = f32[96,320,2,40]{0,3,2,1:T(8,128)} async-done(((f32[96,320,2,40]{0,3,2,1:T(8,128)}), f32[96,320,2,40]{0,3,2,1:T(8,128)}, u32[]{:S(2)}, u32[]{:S(2)}) %all-to-all-start.1) | async-done | bytes 9830432 | tf_op jit(solution)/shard_map/all_to_all | solution.py:73
  1063.2 13.9 %copy.36 = f32[4,96,80,2,40]{1,0,4,3,2:T(4,128)} copy(f32[4,96,80,2,40]{1,4,3,2,0:T(8,128)} %bitcast.12) | data formatting | bytes 19660800 | tf_op jit(solution)/shard_map/all_to_all | solution.py:73
  1077.2 14.3 %reshape.227 = f32[384,6400]{0,1:T(8,128)} reshape(f32[4,96,80,2,40]{1,0,4,3,2:T(4,128)} %copy.36) | data formatting | bytes 19660800 | tf_op jit(solution)/shard_map/reshape | solution.py:82
  1091.5 24.0 %bitcast_multiply_fusion.1 = f32[384,6400]{0,1:T(8,128)S(1)} fusion(f32[384,6400]{0,1:T(8,128)} %reshape.227, f32[384,384]{1,0:T(8,128)S(1)} %copy-done.3, f32[384,80,40]{0,2,1:T(8,128)} %copy-done.2), kind=kOutput, calls=%fused_computation.3 | convolution fusion | flops 11327078400 | bytes 25165824 | tf_op jit(solution)/shard_map/dot_general | solution.py:81
  1115.5 19.0 %fusion.25 = f32[6400,384]{1,0:T(8,128)S(1)} fusion(f32[384,6400]{0,1:T(8,128)S(1)} %bitcast_multiply_fusion.1, f32[384,384]{1,0:T(8,128)S(1)} %copy-done), kind=kOutput, calls=%fused_computation.54 | convolution fusion | flops 11324620800 | bytes 20250624 | tf_op jit(solution)/shard_map/dot_general | solution.py:90
  1134.5 3.9 copy-done.1
  1138.4 8.2 convolution_bitcast_fusion.2
  1147.3 10.6 multiply_add_fusion
  (33 shorter events, 1.8 us)
Async XLA Ops:
  0.0 788.9 %copy-start = (f32[384,384]{1,0:T(8,128)S(1)}, f32[384,384]{1,0:T(8,128)}, u32[]{:S(2)}) copy-start(f32[384,384]{1,0:T(8,128)} %param.13) | copy-start | bytes 1769476
  173.4 347.8 %all-to-all-start = ((f32[96,96,2,320]{1,2,0,3:T(2,128)}), f32[96,96,2,320]{1,2,0,3:T(2,128)}, u32[]{:S(2)}, u32[]{:S(2)}) async-start(f32[96,96,2,320]{1,2,0,3:T(2,128)} %copy.29), calls=%async_computation | async-start | bytes 62914560 | tf_op jit(solution)/shard_map/all_to_all | solution.py:49
  775.6 6.5 copy-start.4
  775.6 7.0 copy-start.7
  775.6 7.0 copy-start.3
  775.6 7.1 copy-start.6
  775.6 287.6 %all-to-all-start.1 = ((f32[96,320,2,40]{0,3,2,1:T(8,128)}), f32[96,320,2,40]{0,3,2,1:T(8,128)}, u32[]{:S(2)}, u32[]{:S(2)}) async-start(f32[96,320,2,40]{0,3,2,1:T(8,128)} %pad_maximum_fusion), calls=%async_computation.1 | async-start | bytes 26214400 | tf_op jit(solution)/shard_map/all_to_all | solution.py:73
  784.0 28.7 %copy-start.2 = (f32[384,80,40]{0,2,1:T(8,128)}, f32[384,80,40]{0,2,1:T(8,128)S(1)}, u32[]{:S(2)}) copy-start(f32[384,80,40]{0,2,1:T(8,128)S(1)} %add_divide_fusion) | copy-start | bytes 14745604
  1115.5 22.9 %copy-start.5 = (f32[2,384]{1,0:T(2,128)S(1)}, f32[2,384]{1,0:T(2,128)}, u32[]{:S(2)}) copy-start(f32[2,384]{1,0:T(2,128)} %param.15) | copy-start | bytes 9220
  1134.5 3.9 copy-start.1
where the time goes:
time: 1170 us; the launch traced here: 1160 us
  waiting for transfers between devices  585 us (50%)
  local copies, waits for them, and re-layouts  301 us (26%)
  matrix products  210 us (18%)
  other arithmetic  47.2 us (4%)
  starting transfers between devices  14.7 us (1%)
    all_to_all x1, waiting for transfers between devices, body(): lax.all_to_all(z_modes, 'px', split_axis=3, concat_axis=1, tiled=True)  339 us
    all_to_all x1, waiting for transfers between devices, body(): lax.all_to_all(forcing, 'py', split_axis=1, concat_axis=0, tiled=True)  246 us
    reshape x2, local copies, waits for them, and re-layouts, body(): z_modes = z_modes.reshape(y_count, x_count, 2, KZ)  96 us
    dot_general x1, matrix products, body(): jnp.einsum('xyn,kn->yxk', product, z_table, precision=highest, preferred_...  73.2 us
    dot_general x1, matrix products, body(): jnp.einsum('kn,ynq->ykq', x_table, flat, precision=highest, preferred_ele...  61.4 us
    unnamed x24, local copies, waits for them, and re-layouts  52.4 us
    reshape x1, local copies, waits for them, and re-layouts, body(): flat = block.reshape(items, NX, 2 * kz_count)  31.2 us
    slice x1, local copies, waits for them, and re-layouts, body(): imag_part = mixed[:, 0, :, 1] - mixed[:, 1, :, 0]  30.9 us
  transfers between devices with their start and end apart: 2, of which 2 were waited for; matrix products, arithmetic and copies ran while one was open for 3% of the time, Pallas kernels for 0%

commit v1 on v0

v1 whole, which is shorter than its diff:
```python
import math

import jax
import jax.numpy as jnp
from jax import lax
from jax.experimental import pallas as pl
from jax.experimental.pallas import tpu as pltpu
from jax.sharding import PartitionSpec as P

HIGH = lax.Precision.HIGH
PARTS = 3
LANES = 128
CHUNKS = 5
VMEM_BYTES = 48 * 1024 * 1024


def dft_tables(length, kept):
    points = jnp.arange(length, dtype=jnp.int32)
    waves = jnp.arange(kept, dtype=jnp.int32) - kept // 2
    turns = waves[:, None] * points[None, :] % length
    angles = turns.astype(jnp.float32) * (2.0 * math.pi / length)
    scale_factor = 1.0 / math.sqrt(length)
    return (jnp.cos(angles) * scale_factor, jnp.sin(angles) * scale_factor)


def make_body(px_size, py_size):
    def body(
        base_flow,
        tangent,
        kx_bounds,
        left_basis,
        right_basis,
        eigenvalues,
        wall_rows,
        sources,
        influence,
    ):
        x_count, y_count, nz = base_flow.shape
        nx = x_count * px_size
        ny = y_count * py_size
        kz_local = influence.shape[2]
        kx_local = influence.shape[1]
        kz_all = kz_local * px_size
        kx_all = kx_local * py_size
        mx = kx_all // 2
        mz = kz_all // 2
        parts = PARTS if (kz_local * (y_count // PARTS)) % 128 == 0 else 1
        rows = y_count // parts

        z_cosine, z_sine = dft_tables(nz, kz_all)
        z_table = jnp.stack(
            [z_cosine.reshape(px_size, kz_local, nz), -z_sine.reshape(px_size, kz_local, nz)],
            axis=1,
        ).reshape(px_size * 2 * kz_local, nz)

        kx_scaled = (jnp.arange(kx_all, dtype=jnp.int32) - mx).astype(jnp.float32) / mx
        x_cosine, x_sine = dft_tables(nx, kx_all)
        x_cosine = x_cosine * kx_scaled[:, None]
        x_sine = x_sine * kx_scaled[:, None]
        to_real = jnp.stack([x_sine, -x_cosine], axis=1)
        to_imag = jnp.stack([x_cosine, x_sine], axis=1)
        x_table = jnp.stack([to_real, to_imag], axis=1)
        x_table = x_table.reshape(kx_all * 2, 2, px_size, x_count)
        x_table = jnp.transpose(x_table, (0, 2, 1, 3)).reshape(kx_all * 2, 2 * nx)

        arrived = []
        for part in range(parts):
            low = part * rows
            product = base_flow[:, low : low + rows] * tangent[:, low : low + rows]
            product = product.reshape(x_count * rows, nz)
            z_modes = lax.dot_general(
                z_table, product, (((1,), (1,)), ((), ())), precision=HIGH,
                preferred_element_type=jnp.float32,
            )
            z_modes = z_modes.reshape(px_size, 2 * kz_local, x_count * rows)
            block = lax.all_to_all(z_modes, "px", split_axis=0, concat_axis=0, tiled=True)
            block = block.reshape(px_size, 2, kz_local, x_count, rows)
            block = jnp.transpose(block, (0, 1, 3, 2, 4)).reshape(2 * nx, kz_local * rows)
            forcing = jnp.dot(
                x_table, block, precision=HIGH, preferred_element_type=jnp.float32
            )
            forcing = forcing.reshape(py_size, kx_local * 2, kz_local * rows)
            forcing = lax.all_to_all(forcing, "py", split_axis=0, concat_axis=0, tiled=True)
            arrived.append(forcing.reshape(py_size, kx_local * 2 * kz_local, rows))
        pieces = jnp.stack(arrived, axis=0)
        pieces = jnp.transpose(pieces, (2, 0, 1, 3)).reshape(kx_local * 2 * kz_local, ny)
        left_here = left_basis.reshape(ny, py_size, parts, rows)
        left_here = jnp.transpose(left_here, (0, 2, 1, 3)).reshape(ny, ny)

        projected = lax.dot_general(
            pieces, left_here, (((1,), (1,)), ((), ())), precision=HIGH,
            preferred_element_type=jnp.float32,
        ).reshape(kx_local, 2, kz_local, ny)

        kx_start = lax.axis_index("py") * kx_local
        kz_start = lax.axis_index("px") * kz_local
        columns = kx_start + jnp.arange(kx_local, dtype=jnp.int32)
        kx_here = (columns - mx).astype(jnp.float32) / mx
        kz_here = (kz_start + jnp.arange(kz_local, dtype=jnp.int32) - mz).astype(jnp.float32) / mz
        bounds = lax.dynamic_slice_in_dim(kx_bounds, kz_start, kz_local, 1)
        keep = (columns[:, None] >= bounds[0][None, :]) & (columns[:, None] < bounds[1][None, :])
        shift = kx_here[:, None] ** 2 + kz_here[None, :] ** 2
        gain = 1.0 / (1.0 + eigenvalues[None, None, None, :] + shift[:, None, :, None])
        highest = lax.Precision.HIGHEST
        source_proj = jnp.dot(
            sources, left_basis.T, precision=highest, preferred_element_type=jnp.float32
        )
        wall_map = jnp.dot(
            wall_rows, right_basis, precision=highest, preferred_element_type=jnp.float32
        )
        weighted = jnp.where(keep[:, None, :, None], gain * projected, 0.0)
        wall_values = lax.dot_general(
            wall_map, weighted.reshape(-1, ny), (((1,), (1,)), ((), ())), precision=HIGH,
            preferred_element_type=jnp.float32,
        ).reshape(2, kx_local, 2, kz_local)
        inverse_map = influence.reshape(2, 2, kx_local, 1, kz_local)
        first = -(inverse_map[0, 0] * wall_values[0] + inverse_map[0, 1] * wall_values[1])
        second = -(inverse_map[1, 0] * wall_values[0] + inverse_map[1, 1] * wall_values[1])
        total = weighted + gain * (
            first[..., None] * source_proj[0] + second[..., None] * source_proj[1]
        )
        response = lax.dot_general(
            total.reshape(-1, ny), right_basis, (((1,), (1,)), ((), ())), precision=HIGH,
            preferred_element_type=jnp.float32,
        ).reshape(kx_local, 2, kz_local, ny)
        return jnp.transpose(response, (3, 0, 1, 2))

    return body


def split(value):
    high = value.astype(jnp.bfloat16)
    low = (value - high.astype(jnp.float32)).astype(jnp.bfloat16)
    return high, low


def split_table(value):
    rounded = lax.reduce_precision(value, exponent_bits=8, mantissa_bits=7)
    return rounded.astype(jnp.bfloat16), (value - rounded).astype(jnp.bfloat16)


def dot3(a, b, dims):
    def one(u, v):
        return lax.dot_general(u, v, (dims, ((), ())), preferred_element_type=jnp.float32)

    return one(a[0], b[1]) + one(a[1], b[0]) + one(a[0], b[0])


def z_kernel(groups, high_ref, low_ref, base_ref, tangent_ref, *out_refs):
    step, y_count, nz = base_ref.shape
    product = (base_ref[...] * tangent_ref[...]).reshape(step * y_count, nz)
    modes = dot3((high_ref[...], low_ref[...]), split(product), ((1,), (1,)))
    rows = out_refs[0].shape[0]
    for chunk, out_ref in enumerate(out_refs):
        tiles = out_ref.shape[1]
        flat = out_ref.reshape(rows * tiles * step, LANES)
        for x in range(step):
            pieces = []
            for group in range(groups):
                low = (chunk * groups + group) * rows
                pieces.append(modes[low : low + rows, x * y_count : (x + 1) * y_count])
            whole = jnp.concatenate(pieces, axis=1)
            for tile in range(tiles):
                flat[pl.ds(tile * step + x, rows, stride=tiles * step), :] = whole[
                    :, tile * LANES : (tile + 1) * LANES
                ]


def x_kernel(high_ref, low_ref, data_ref, *out_refs):
    owners, _, parts, tiles, x_count, _ = data_ref.shape
    data = jnp.concatenate(
        [data_ref[:, 0, :, tile].reshape(owners * parts * x_count, LANES) for tile in range(tiles)],
        axis=1,
    )
    forcing = dot3((high_ref[...], low_ref[...]), split(data), ((1,), (0,)))
    rows = out_refs[0].shape[1]
    for ahead, out_ref in enumerate(out_refs):
        out_ref[0] = forcing[ahead * rows : (ahead + 1) * rows]


def wall_kernel(groups, chunks, py_size, *refs):
    data_refs = refs[: chunks * py_size]
    (aux_ref, lane_ref, left_high, left_low, right_high, right_low, out_ref, turned) = refs[
        chunks * py_size :
    ]
    per_chunk, rows, lanes = data_refs[0].shape
    y_count = lanes // groups
    profiles = []
    for chunk in range(chunks):
        for q in range(per_chunk):
            parts = [ref[q] for ref in data_refs[chunk * py_size : (chunk + 1) * py_size]]
            for group in range(groups):
                cut = slice(group * y_count, (group + 1) * y_count)
                profiles.append(jnp.concatenate([part[:, cut] for part in parts], axis=1))
    profiles = jnp.concatenate(profiles, axis=0)
    projected = dot3(
        split(profiles), (left_high[...], left_low[...]), ((1,), (1,))
    )
    aux = aux_ref[...]
    gain = 1.0 / (1.0 + lane_ref[0:1, :] + aux[:, 0:1])
    weighted = jnp.where(aux[:, 1:2] > 0.5, gain * projected, 0.0)
    wall_0 = jnp.sum(weighted * lane_ref[1:2, :], axis=1, keepdims=True)
    wall_1 = jnp.sum(weighted * lane_ref[2:3, :], axis=1, keepdims=True)
    first = -(aux[:, 2:3] * wall_0 + aux[:, 3:4] * wall_1)
    second = -(aux[:, 4:5] * wall_0 + aux[:, 5:6] * wall_1)
    total = weighted + gain * (first * lane_ref[3:4, :] + second * lane_ref[4:5, :])
    response = dot3(split(total), (right_high[...], right_low[...]), ((1,), (1,)))
    kz_count = chunks * per_chunk * groups
    for tile in range(turned.shape[0]):
        cut = slice(tile * LANES, (tile + 1) * LANES)
        for kz in range(kz_count):
            turned[tile, pl.ds(kz, rows, stride=kz_count), :] = response[
                kz * rows : (kz + 1) * rows, cut
            ]
        out_ref[:, :, cut] = turned[tile].reshape(rows, kz_count, LANES)


def make_kernel_body(px_size, py_size, groups):
    def body(
        base_flow,
        tangent,
        kx_bounds,
        left_basis,
        right_basis,
        eigenvalues,
        wall_rows,
        sources,
        influence,
    ):
        x_count, y_count, nz = base_flow.shape
        nx = x_count * px_size
        ny = y_count * py_size
        kz_local = influence.shape[2]
        kx_local = influence.shape[1]
        kz_all = kz_local * px_size
        kx_all = kx_local * py_size
        mx = kx_all // 2
        mz = kz_all // 2
        quarter = kz_local // groups
        chunks = CHUNKS if quarter % CHUNKS == 0 else 1
        per_chunk = quarter // chunks
        lanes = groups * y_count
        tiles = lanes // LANES
        params = pltpu.CompilerParams(vmem_limit_bytes=VMEM_BYTES)

        z_cosine, z_sine = dft_tables(nz, kz_all)
        z_table = jnp.stack([z_cosine, -z_sine], axis=1)
        z_table = z_table.reshape(px_size, chunks, per_chunk, groups, 2, nz)
        z_table = jnp.transpose(z_table, (1, 3, 0, 2, 4, 5)).reshape(2 * kz_all, nz)
        z_high, z_low = split_table(z_table)

        kx_scaled = (jnp.arange(kx_all, dtype=jnp.int32) - mx).astype(jnp.float32) / mx
        x_cosine, x_sine = dft_tables(nx, kx_all)
        x_cosine = x_cosine * kx_scaled[:, None]
        x_sine = x_sine * kx_scaled[:, None]
        to_real = jnp.stack([x_sine, -x_cosine], axis=1)
        to_imag = jnp.stack([x_cosine, x_sine], axis=1)
        x_table = jnp.stack([to_real, to_imag], axis=1)
        x_table = x_table.reshape(kx_all * 2, 2, px_size, x_count)
        x_table = jnp.transpose(x_table, (0, 2, 1, 3)).reshape(kx_all * 2, 2 * nx)
        here = lax.axis_index("py")
        order = (here + jnp.arange(py_size, dtype=jnp.int32)) % py_size
        x_table = jnp.take(x_table.reshape(py_size, 2 * kx_local, 2 * nx), order, axis=0)
        x_table = x_table.reshape(kx_all * 2, 2 * nx)
        x_high, x_low = split_table(x_table)

        step = 8
        rows = px_size * per_chunk * 2
        full = pl.BlockSpec(z_table.shape, lambda i: (0, 0))
        grid_block = pl.BlockSpec((step, y_count, nz), lambda i: (i, 0, 0))
        z_modes = pl.pallas_call(
            lambda *refs: z_kernel(groups, *refs),
            grid=(x_count // step,),
            in_specs=[full, full, grid_block, grid_block],
            out_specs=[pl.BlockSpec((rows, tiles, step, LANES), lambda i: (0, 0, i, 0))] * chunks,
            out_shape=[jax.ShapeDtypeStruct((rows, tiles, x_count, LANES), jnp.float32)] * chunks,
            compiler_params=params,
            cost_estimate=pl.CostEstimate(
                flops=6 * 2 * kz_all * x_count * y_count * nz,
                bytes_accessed=4 * (2 * x_count * y_count * nz + 2 * kz_all * x_count * y_count),
                transcendentals=0,
            ),
            name="z_modes",
        )(z_high, z_low, base_flow, tangent)

        arrived = []
        made = []
        for chunk in range(chunks):
            ready = z_modes[chunk]
            if chunk >= 2:
                ready, made[chunk - 2] = lax.optimization_barrier((ready, made[chunk - 2]))
            block = lax.all_to_all(ready, "px", split_axis=0, concat_axis=0, tiled=True)
            block = block.reshape(px_size, per_chunk, 2, tiles, x_count, LANES)
            full = pl.BlockSpec(x_table.shape, lambda i: (0, 0))
            forcing = pl.pallas_call(
                x_kernel,
                grid=(per_chunk,),
                in_specs=[
                    full,
                    full,
                    pl.BlockSpec(
                        (px_size, 1, 2, tiles, x_count, LANES), lambda i: (0, i, 0, 0, 0, 0)
                    ),
                ],
                out_specs=[pl.BlockSpec((1, 2 * kx_local, lanes), lambda i: (i, 0, 0))] * py_size,
                out_shape=[
                    jax.ShapeDtypeStruct((per_chunk, 2 * kx_local, lanes), jnp.float32)
                ]
                * py_size,
                compiler_params=params,
                cost_estimate=pl.CostEstimate(
                    flops=6 * 2 * kx_all * 2 * nx * per_chunk * lanes,
                    bytes_accessed=4 * (2 * nx + 2 * kx_all) * per_chunk * lanes,
                    transcendentals=0,
                ),
                name="x_modes",
            )(x_high, x_low, block)
            made.append(forcing[0])
            arrived.append(forcing[0])
            for ahead in range(1, py_size):
                pairs = [(j, (j + ahead) % py_size) for j in range(py_size)]
                arrived.append(lax.ppermute(forcing[ahead], "py", pairs))

        kx_start = lax.axis_index("py") * kx_local
        kz_start = lax.axis_index("px") * kz_local
        columns = kx_start + jnp.arange(kx_local, dtype=jnp.int32)
        kx_here = (columns - mx).astype(jnp.float32) / mx
        kz_here = (kz_start + jnp.arange(kz_local, dtype=jnp.int32) - mz).astype(jnp.float32) / mz
        bounds = lax.dynamic_slice_in_dim(kx_bounds, kz_start, kz_local, 1)
        keep = (columns[:, None] >= bounds[0][None, :]) & (columns[:, None] < bounds[1][None, :])
        shift = kx_here[:, None] ** 2 + kz_here[None, :] ** 2
        blank = jnp.zeros_like(shift)
        aux = jnp.stack(
            [shift, keep.astype(jnp.float32)] + [influence[i] for i in range(4)] + [blank] * 2, axis=-1
        )
        kx_step = 8
        kx_blocks = kx_local // kx_step
        aux = jnp.transpose(aux.reshape(kx_blocks, kx_step, kz_local, 8), (0, 2, 1, 3))
        aux = jnp.broadcast_to(aux[:, :, :, None], (kx_blocks, kz_local, kx_step, 2, 8))
        aux = aux.reshape(-1, 8)
        highest = lax.Precision.HIGHEST
        source_proj = jnp.dot(
            sources, left_basis.T, precision=highest, preferred_element_type=jnp.float32
        )
        wall_map = jnp.dot(
            wall_rows, right_basis, precision=highest, preferred_element_type=jnp.float32
        )
        lane_rows = jnp.concatenate(
            [eigenvalues[None], wall_map, source_proj, jnp.zeros((3, ny), jnp.float32)], axis=0
        )
        behind = (here - jnp.arange(py_size, dtype=jnp.int32)) % py_size
        left_here = jnp.take(left_basis.reshape(ny, py_size, y_count), behind, axis=1)
        left_here = left_here.reshape(ny, ny)
        left_high, left_low = split_table(left_here)
        right_high, right_low = split_table(right_basis)
        square = pl.BlockSpec((ny, ny), lambda i: (0, 0))
        block_rows = kz_local * kx_step * 2
        response = pl.pallas_call(
            lambda *refs: wall_kernel(groups, chunks, py_size, *refs),
            grid=(kx_blocks,),
            in_specs=[
                pl.BlockSpec((per_chunk, 2 * kx_step, lanes), lambda i: (0, i, 0))
            ]
            * (chunks * py_size)
            + [
                pl.BlockSpec((block_rows, 8), lambda i: (i, 0)),
                pl.BlockSpec((8, ny), lambda i: (0, 0)),
                square,
                square,
                square,
                square,
            ],
            out_specs=pl.BlockSpec((2 * kx_step, kz_local, ny), lambda i: (i, 0, 0)),
            out_shape=jax.ShapeDtypeStruct((2 * kx_local, kz_local, ny), jnp.float32),
            scratch_shapes=[pltpu.VMEM((ny // LANES, block_rows, LANES), jnp.float32)],
            compiler_params=params,
            cost_estimate=pl.CostEstimate(
                flops=12 * 2 * kx_local * kz_local * ny * ny,
                bytes_accessed=4 * 4 * kx_local * kz_local * ny,
                transcendentals=0,
            ),
            name="wall_normal",
        )(*arrived, aux, lane_rows, left_high, left_low, right_high, right_low)
        response = response.reshape(kx_local, 2, kz_local, ny)
        return jnp.transpose(response, (3, 0, 1, 2))

    return body


def lane_groups(y_count):
    return LANES * y_count // math.gcd(LANES, y_count) // y_count


def solution(mesh):
    px_size = mesh.shape["px"]
    py_size = mesh.shape["py"]

    def body(*arrays):
        x_count, y_count, _ = arrays[0].shape
        kx_local, kz_local = arrays[8].shape[1:]
        groups = lane_groups(y_count)
        fits = (
            x_count % 8 == 0
            and y_count % 8 == 0
            and kx_local % 8 == 0
            and kz_local % 8 == 0
            and kz_local % groups == 0
            and y_count * py_size % LANES == 0
        )
        if fits:
            return make_kernel_body(px_size, py_size, groups)(*arrays)
        return make_body(px_size, py_size)(*arrays)

    placed = (
        P("px", "py", None),
        P("px", "py", None),
        P(),
        P(),
        P(),
        P(),
        P(),
        P(),
        P(None, "py", "px"),
    )
    return jax.shard_map(
        body,
        mesh=mesh,
        in_specs=placed,
        out_specs=P(None, "py", None, "px"),
        check_vma=False,
    )
```

time: 1170 us -> 581 us (0.50)
  waiting for transfers between devices: 585 us -> 221 us
  local copies, waits for them, and re-layouts: 301 us -> 77.9 us
  matrix products: 210 us -> 3.08 us
  Pallas kernels: 0 us -> 135 us
  blocking collectives: 0 us -> 58.4 us
  starting transfers between devices: 14.7 us -> 59.3 us
  other arithmetic: 47.2 us -> 17.2 us
    all_to_all x2 -> x4, waiting for transfers between devices: 585 us -> 83.2 us  [body(): block = lax.all_to_all(ready, 'px', split_axis=0, concat_axis=0, tiled=True)]
    dot_general x7 -> x2, matrix products: 210 us -> 3.08 us  [the longest x1 1.67 us: body(): jnp.dot(sources, left_basis.T, precision=highest, preferred_element_type=...]
    reshape x5 -> x2, local copies, waits for them, and re-layouts: 169 us -> 9.88 us  [the longest x1 7.26 us: body(): x_table = x_table.reshape(kx_all * 2, 2, px_size, x_count)]
    ppermute x0 -> x15, waiting for transfers between devices: none -> 137 us  [body(): arrived.append(lax.ppermute(forcing[ahead], 'py', pairs))]
    pallas_call x0 -> x7, Pallas kernels: none -> 135 us  [the longest x1 49.4 us: body(): pl.pallas_call(lambda *refs: wall_kernel(groups, chunks, py_size, *refs),...]
    all_to_all x0 -> x1, blocking collectives: none -> 58.4 us  [body(): block = lax.all_to_all(ready, 'px', split_axis=0, concat_axis=0, tiled=True)]
    all_to_all x3 -> x0, local copies, waits for them, and re-layouts: 42.4 us -> none  [the longest x2 28.4 us: body(): lax.all_to_all(z_modes, 'px', split_axis=3, concat_axis=1, tiled=True)]
    ppermute x0 -> x15, starting transfers between devices: none -> 34.9 us  [body(): arrived.append(lax.ppermute(forcing[ahead], 'py', pairs))]
  transfers between devices with their start and end apart: 2 -> 19, of which waited for: 2 -> 13; matrix products, arithmetic and copies ran while one was open for 3% -> 11% of each run, Pallas kernels for 0% -> 8%
where the time goes in v1:
time: 581 us; the launch traced here: 572 us
  waiting for transfers between devices  221 us (38%)
  Pallas kernels  135 us (23%)
  local copies, waits for them, and re-layouts  77.9 us (13%)
  starting transfers between devices  59.3 us (10%)
  blocking collectives  58.4 us (10%)
  other arithmetic  17.2 us (3%)
    ppermute x15, waiting for transfers between devices, body(): arrived.append(lax.ppermute(forcing[ahead], 'py', pairs))  137 us
    all_to_all x4, waiting for transfers between devices, body(): block = lax.all_to_all(ready, 'px', split_axis=0, concat_axis=0, tiled=True)  83.2 us
    all_to_all x1, blocking collectives, body(): block = lax.all_to_all(ready, 'px', split_axis=0, concat_axis=0, tiled=True)  58.4 us
    pallas_call x1, Pallas kernels, body(): pl.pallas_call(lambda *refs: wall_kernel(groups, chunks, py_size, *refs),...  49.4 us
    pallas_call x5, Pallas kernels, body(): pl.pallas_call(x_kernel, grid=(per_chunk,), in_specs=[full, full, pl.Bloc...  44.6 us
    pallas_call x1, Pallas kernels, body(): pl.pallas_call(lambda *refs: z_kernel(groups, *refs), grid=(x_count // st...  40.7 us
    ppermute x15, starting transfers between devices, body(): arrived.append(lax.ppermute(forcing[ahead], 'py', pairs))  34.9 us
    unnamed x71, local copies, waits for them, and re-layouts  24.9 us
  transfers between devices with their start and end apart: 19, of which 13 were waited for; matrix products, arithmetic and copies ran while one was open for 11% of the time, Pallas kernels for 8%

profile of v1, /device:TPU:11, one launch (start us, length us, event | category | flops | bytes accessed | tf_op | source)
XLA Modules:
  0.0 571.8 jit_solution(13870508837125711187)
XLA Ops:
  0.0 4.1 cosine_multiply_fusion
  9.6 40.7 %z_modes.1 = (f32[32,3,96,128]{3,2,1,0:T(8,128)}, f32[32,3,96,128]{3,2,1,0:T(8,128)}, f32[32,3,96,128]{3,2,1,0:T(8,128)}, f32[32,3,96,128]{3,2,1,0:T(8,128)}, f32[32,3,96,128]{3,2,1,0:T(8,128)}) custom-call(bf16[640,768]{1,0:T(8,128)(2,1)S(1)} %get-tuple-element.64.refs_0_, bf16[640,768]{1,0:T(8,128)(2,1)S(1)} %get-tuple-element.63.refs_1_, ...), custom_call_target="tpu_custom_call" | custom-call | flops 27179089920 | bytes 80216064 | tf_op jit(solution)/shard_map/z_modes/pallas_call | solution.py:271
  50.3 58.4 %all_to_all.25 = f32[32,3,96,128]{3,2,1,0:T(8,128)} all-to-all(f32[32,3,96,128]{3,2,1,0:T(8,128)} %get-tuple-element.33), channel_id=1, replica_groups=mesh['px'=8,'py'=4] {'px'}, dimensions={0} | all-to-all | bytes 9437184 | tf_op jit(solution)/shard_map/all_to_all | solution.py:292
  108.6 6.4 %all-to-all-start.1 = ((f32[32,3,96,128]{3,2,1,0:T(8,128)}), f32[32,3,96,128]{3,2,1,0:T(8,128)}, u32[]{:S(2)}, u32[]{:S(2)}) async-start(f32[32,3,96,128]{3,2,1,0:T(8,128)} %get-tuple-element.38), calls=%async_computation.1 | async-start | bytes 9437184 | tf_op jit(solution)/shard_map/all_to_all | solution.py:292
  115.1 4.1 fusion.14
  119.9 4.9 copy.39
  124.8 7.3 %reshape.489 = f32[640,2,8,96]{3,2,1,0:T(8,128)} reshape(f32[320,2,2,768]{3,2,1,0:T(2,128)} %copy.39) | data formatting | bytes 7864320 | tf_op jit(solution)/shard_map/reshape | solution.py:259
  132.1 7.5 %copy.40 = f32[640,8,2,96]{3,2,1,0:T(2,128)} copy(f32[640,8,2,96]{3,1,2,0:T(8,128)} %bitcast.52) | data formatting | bytes 7864320 | tf_op jit(solution)/shard_map/transpose | solution.py:260
  139.6 8.5 %reshape_reshape.3 = f32[4,160,1536]{2,1,0:T(8,128)} reshape(f32[640,8,2,96]{3,2,1,0:T(2,128)} %copy.40) | data formatting | bytes 7864320 | tf_op jit(solution)/shard_map/reshape;reshape | solution.py:263
  149.4 4.8 gather_fusion
  157.0 9.6 %x_modes.5 = (f32[2,160,384]{2,1,0:T(8,128)S(1)}, f32[2,160,384]{2,1,0:T(8,128)S(1)}, f32[2,160,384]{2,1,0:T(8,128)S(1)}, f32[2,160,384]{2,1,0:T(8,128)}) custom-call(bf16[640,1536]{1,0:T(8,128)(2,1)S(1)} %get-tuple-element.62.high_ref, bf16[640,1536]{1,0:T(8,128)(2,1)S(1)} %get-tuple-element.61.low_ref, f32[8,2,2,3,96,128]{5,4,3,2,1,0:T(8,128)} %bitcast.53), custom_call_target="tpu_custom_call" | custom-call | flops 4529848320 | bytes 6684672 | tf_op jit(solution)/shard_map/x_modes/pallas_call | solution.py:295
  168.9 5.5 all-to-all-start.2
  175.9 8.2 %x_modes.6 = (f32[2,160,384]{2,1,0:T(8,128)S(1)}, f32[2,160,384]{2,1,0:T(8,128)S(1)}, f32[2,160,384]{2,1,0:T(8,128)S(1)}, f32[2,160,384]{2,1,0:T(8,128)S(1)}) custom-call(bf16[640,1536]{1,0:T(8,128)(2,1)S(1)} %copy-done.2, bf16[640,1536]{1,0:T(8,128)(2,1)S(1)} %get-tuple-element.61.low_ref, f32[8,2,2,3,96,128]{5,4,3,2,1,0:T(8,128)} %bitcast.7.data_ref), custom_call_target="tpu_custom_call" | custom-call | flops 4529848320 | bytes 6684672 | tf_op jit(solution)/shard_map/x_modes/pallas_call | solution.py:295
  187.3 40.3 %all-to-all-done.2 = f32[32,3,96,128]{3,2,1,0:T(8,128)} async-done(((f32[32,3,96,128]{3,2,1,0:T(8,128)}), f32[32,3,96,128]{3,2,1,0:T(8,128)}, u32[]{:S(2)}, u32[]{:S(2)}) %all-to-all-start.2) | async-done | bytes 4718624 | tf_op jit(solution)/shard_map/all_to_all | solution.py:292
  227.6 6.1 %all-to-all-start.3 = ((f32[32,3,96,128]{3,2,1,0:T(8,128)}), f32[32,3,96,128]{3,2,1,0:T(8,128)}, u32[]{:S(2)}, u32[]{:S(2)}) async-start(f32[32,3,96,128]{3,2,1,0:T(8,128)} %get-tuple-element.50), calls=%async_computation.3 | async-start | bytes 9437184 | tf_op jit(solution)/shard_map/all_to_all | solution.py:292
  235.3 8.8 %x_modes.7 = (f32[2,160,384]{2,1,0:T(8,128)S(1)}, f32[2,160,384]{2,1,0:T(8,128)}, f32[2,160,384]{2,1,0:T(8,128)S(1)}, f32[2,160,384]{2,1,0:T(8,128)S(1)}) custom-call(bf16[640,1536]{1,0:T(8,128)(2,1)S(1)} %copy-done.3, bf16[640,1536]{1,0:T(8,128)(2,1)S(1)} %get-tuple-element.61.low_ref, f32[8,2,2,3,96,128]{5,4,3,2,1,0:T(8,128)} %bitcast.8.data_ref), custom_call_target="tpu_custom_call" | custom-call | flops 4529848320 | bytes 6684672 | tf_op jit(solution)/shard_map/x_modes/pallas_call | solution.py:295
  244.1 42.9 %all-to-all-done.3 = f32[32,3,96,128]{3,2,1,0:T(8,128)} async-done(((f32[32,3,96,128]{3,2,1,0:T(8,128)}), f32[32,3,96,128]{3,2,1,0:T(8,128)}, u32[]{:S(2)}, u32[]{:S(2)}) %all-to-all-start.3) | async-done | bytes 4718624 | tf_op jit(solution)/shard_map/all_to_all | solution.py:292
  287.0 6.4 %all-to-all-start.4 = ((f32[32,3,96,128]{3,2,1,0:T(8,128)}), f32[32,3,96,128]{3,2,1,0:T(8,128)}, u32[]{:S(2)}, u32[]{:S(2)}) async-start(f32[32,3,96,128]{3,2,1,0:T(8,128)} %get-tuple-element.56), calls=%async_computation.4 | async-start | bytes 9437184 | tf_op jit(solution)/shard_map/all_to_all | solution.py:292
  308.4 9.0 %x_modes.8 = (f32[2,160,384]{2,1,0:T(8,128)S(1)}, f32[2,160,384]{2,1,0:T(8,128)}, f32[2,160,384]{2,1,0:T(8,128)}, f32[2,160,384]{2,1,0:T(8,128)}) custom-call(bf16[640,1536]{1,0:T(8,128)(2,1)S(1)} %copy-done.4, bf16[640,1536]{1,0:T(8,128)(2,1)S(1)} %get-tuple-element.61.low_ref, f32[8,2,2,3,96,128]{5,4,3,2,1,0:T(8,128)} %bitcast.9.data_ref), custom_call_target="tpu_custom_call" | custom-call | flops 4529848320 | bytes 6684672 | tf_op jit(solution)/shard_map/x_modes/pallas_call | solution.py:295
  319.0 24.4 %collective-permute-done.4.refs_6_ = f32[2,160,384]{2,1,0:T(8,128)S(1)} collective-permute-done((f32[2,160,384]{2,1,0:T(8,128)}, f32[2,160,384]{2,1,0:T(8,128)S(1)}, u32[]{:S(2)}, u32[]{:S(2)}) %collective-permute-start.4) | collective-permute-done | bytes 491552 | tf_op jit(solution)/shard_map/ppermute | solution.py:322
  347.3 19.9 %collective-permute-done.5.refs_7_ = f32[2,160,384]{2,1,0:T(8,128)S(1)} collective-permute-done((f32[2,160,384]{2,1,0:T(8,128)}, f32[2,160,384]{2,1,0:T(8,128)S(1)}, u32[]{:S(2)}, u32[]{:S(2)}) %collective-permute-start.5) | collective-permute-done | bytes 491552 | tf_op jit(solution)/shard_map/ppermute | solution.py:322
  368.0 28.1 %collective-permute-done.refs_1_ = f32[2,160,384]{2,1,0:T(8,128)S(1)} collective-permute-done((f32[2,160,384]{2,1,0:T(8,128)}, f32[2,160,384]{2,1,0:T(8,128)S(1)}, u32[]{:S(2)}, u32[]{:S(2)}) %collective-permute-start) | collective-permute-done | bytes 491552 | tf_op jit(solution)/shard_map/ppermute | solution.py:322
  399.0 7.6 %collective-permute-done.1.refs_2_ = f32[2,160,384]{2,1,0:T(8,128)S(1)} collective-permute-done((f32[2,160,384]{2,1,0:T(8,128)}, f32[2,160,384]{2,1,0:T(8,128)S(1)}, u32[]{:S(2)}, u32[]{:S(2)}) %collective-permute-start.1) | collective-permute-done | bytes 491552 | tf_op jit(solution)/shard_map/ppermute | solution.py:322
  409.7 9.0 %x_modes.9 = (f32[2,160,384]{2,1,0:T(8,128)S(1)}, f32[2,160,384]{2,1,0:T(8,128)}, f32[2,160,384]{2,1,0:T(8,128)}, f32[2,160,384]{2,1,0:T(8,128)}) custom-call(bf16[640,1536]{1,0:T(8,128)(2,1)S(1)} %copy-done.5, bf16[640,1536]{1,0:T(8,128)(2,1)S(1)} %get-tuple-element.61.low_ref, f32[8,2,2,3,96,128]{5,4,3,2,1,0:T(8,128)} %bitcast.10.data_ref), custom_call_target="tpu_custom_call" | custom-call | flops 4529848320 | bytes 6684672 | tf_op jit(solution)/shard_map/x_modes/pallas_call | solution.py:295
  422.5 19.4 %collective-permute-start.8 = (f32[2,160,384]{2,1,0:T(8,128)S(1)}, f32[2,160,384]{2,1,0:T(8,128)}, u32[]{:S(2)}, u32[]{:S(2)}) collective-permute-start(f32[2,160,384]{2,1,0:T(8,128)S(1)} %get-tuple-element.48), channel_id=1, source_target_pairs={{0,3},{1,0},{2,1},{3,2},{4,7},{5,4},{6,5},{7,6},{8,11},{9,8},{10,9... | collective-permute-start | bytes 1474568 | tf_op jit(solution)/shard_map/ppermute | solution.py:322
  441.9 9.3 %collective-permute-done.11.refs_15_ = f32[2,160,384]{2,1,0:T(8,128)} collective-permute-done((f32[2,160,384]{2,1,0:T(8,128)}, f32[2,160,384]{2,1,0:T(8,128)}, u32[]{:S(2)}, u32[]{:S(2)}) %collective-permute-start.11) | collective-permute-done | bytes 491552 | tf_op jit(solution)/shard_map/ppermute | solution.py:322
  451.3 8.0 %collective-permute-done.6.refs_9_ = f32[2,160,384]{2,1,0:T(8,128)} collective-permute-done((f32[2,160,384]{2,1,0:T(8,128)}, f32[2,160,384]{2,1,0:T(8,128)}, u32[]{:S(2)}, u32[]{:S(2)}) %collective-permute-start.6) | collective-permute-done | bytes 491552 | tf_op jit(solution)/shard_map/ppermute | solution.py:322
  474.6 16.2 %collective-permute-done.7.refs_10_ = f32[2,160,384]{2,1,0:T(8,128)} collective-permute-done((f32[2,160,384]{2,1,0:T(8,128)S(1)}, f32[2,160,384]{2,1,0:T(8,128)}, u32[]{:S(2)}, u32[]{:S(2)}) %collective-permute-start.7) | collective-permute-done | bytes 491552 | tf_op jit(solution)/shard_map/ppermute | solution.py:322
  493.5 8.0 %collective-permute-done.12.refs_17_ = f32[2,160,384]{2,1,0:T(8,128)} collective-permute-done((f32[2,160,384]{2,1,0:T(8,128)}, f32[2,160,384]{2,1,0:T(8,128)}, u32[]{:S(2)}, u32[]{:S(2)}) %collective-permute-start.12) | collective-permute-done | bytes 491552 | tf_op jit(solution)/shard_map/ppermute | solution.py:322
  501.5 10.5 %collective-permute-done.13.refs_18_ = f32[2,160,384]{2,1,0:T(8,128)} collective-permute-done((f32[2,160,384]{2,1,0:T(8,128)}, f32[2,160,384]{2,1,0:T(8,128)}, u32[]{:S(2)}, u32[]{:S(2)}) %collective-permute-start.13) | collective-permute-done | bytes 491552 | tf_op jit(solution)/shard_map/ppermute | solution.py:322
  514.5 4.3 broadcast_in_dim.54
  521.9 49.4 %wall_normal.1 = f32[160,40,384]{2,1,0:T(8,128)} custom-call(f32[2,160,384]{2,1,0:T(8,128)S(1)} %copy-done.22, f32[2,160,384]{2,1,0:T(8,128)S(1)} %copy-done.13, f32[2,160,384]{2,1,0:T(8,128)S(1)} %copy-done.15, f32[2,160,384]{2,1,0:T(8,128)} %collective-permute-done.2.refs_3_, f32[2,160,384]{2,1,0:T(8,128)S(1)} %copy-done.24, f32[2,160,384]{2,1,0:T(8,128)S(1)} %copy-done.7, ...), custom_call_target="tpu_custom_call" | custom-call | flops 11324620800 | bytes 19660800 | tf_op jit(solution)/shard_map/wall_normal/pallas_call | solution.py:358
  (132 shorter events, 73.3 us)
Async XLA Ops:
  0.0 295.5 %copy-start = (f32[2,384]{1,0:T(2,128)S(1)}, f32[2,384]{1,0:T(2,128)}, u32[]{:S(2)}) copy-start(f32[2,384]{1,0:T(2,128)} %param.15) | copy-start | bytes 9220
  108.6 60.3 %all-to-all-start.1 = ((f32[32,3,96,128]{3,2,1,0:T(8,128)}), f32[32,3,96,128]{3,2,1,0:T(8,128)}, u32[]{:S(2)}, u32[]{:S(2)}) async-start(f32[32,3,96,128]{3,2,1,0:T(8,128)} %get-tuple-element.38), calls=%async_computation.1 | async-start | bytes 9437184 | tf_op jit(solution)/shard_map/all_to_all | solution.py:292
  156.9 9.6 %copy-start.1 = (bf16[640,1536]{1,0:T(8,128)(2,1)}, bf16[640,1536]{1,0:T(8,128)(2,1)S(1)}, u32[]{:S(2)}) copy-start(bf16[640,1536]{1,0:T(8,128)(2,1)S(1)} %get-tuple-element.62.high_ref) | copy-start | bytes 5898244
  168.9 58.7 %all-to-all-start.2 = ((f32[32,3,96,128]{3,2,1,0:T(8,128)}), f32[32,3,96,128]{3,2,1,0:T(8,128)}, u32[]{:S(2)}, u32[]{:S(2)}) async-start(f32[32,3,96,128]{3,2,1,0:T(8,128)} %get-tuple-element.44), calls=%async_computation.2 | async-start | bytes 9437184 | tf_op jit(solution)/shard_map/all_to_all | solution.py:292
  227.6 59.4 %all-to-all-start.3 = ((f32[32,3,96,128]{3,2,1,0:T(8,128)}), f32[32,3,96,128]{3,2,1,0:T(8,128)}, u32[]{:S(2)}, u32[]{:S(2)}) async-start(f32[32,3,96,128]{3,2,1,0:T(8,128)} %get-tuple-element.50), calls=%async_computation.3 | async-start | bytes 9437184 | tf_op jit(solution)/shard_map/all_to_all | solution.py:292
  244.1 42.9 %copy-start.25 = (f32[2,160,384]{2,1,0:T(8,128)}, f32[2,160,384]{2,1,0:T(8,128)S(1)}, u32[]{:S(2)}) copy-start(f32[2,160,384]{2,1,0:T(8,128)S(1)} %get-tuple-element.45.refs_8_) | copy-start | bytes 1474564
  244.1 50.7 %copy-start.29 = (f32[4,80,40]{1,2,0:T(8,128)S(1)}, f32[4,80,40]{1,2,0:T(8,128)}, u32[]{:S(2)}) copy-start(f32[4,80,40]{1,2,0:T(8,128)} %param.17) | copy-start | bytes 153604
  244.1 52.8 %copy-start.30 = (f32[2,384]{1,0:T(2,128)S(1)}, f32[2,384]{1,0:T(2,128)}, u32[]{:S(2)}) copy-start(f32[2,384]{1,0:T(2,128)} %param.16) | copy-start | bytes 9220
  287.0 121.1 %all-to-all-start.4 = ((f32[32,3,96,128]{3,2,1,0:T(8,128)}), f32[32,3,96,128]{3,2,1,0:T(8,128)}, u32[]{:S(2)}, u32[]{:S(2)}) async-start(f32[32,3,96,128]{3,2,1,0:T(8,128)} %get-tuple-element.56), calls=%async_computation.4 | async-start | bytes 9437184 | tf_op jit(solution)/shard_map/all_to_all | solution.py:292
  299.8 18.3 %collective-permute-start.3 = (f32[2,160,384]{2,1,0:T(8,128)}, f32[2,160,384]{2,1,0:T(8,128)S(1)}, u32[]{:S(2)}, u32[]{:S(2)}) collective-permute-start(f32[2,160,384]{2,1,0:T(8,128)} %copy-done.20), channel_id=1, source_target_pairs={{0,1},{1,2},{2,3},{3,0},{4,5},{5,6},{6,7},{7,4},{8,9},{9,10},{10,1... | collective-permute-start | bytes 1474568 | tf_op jit(solution)/shard_map/ppermute | solution.py:322
  301.2 42.2 %collective-permute-start.4 = (f32[2,160,384]{2,1,0:T(8,128)}, f32[2,160,384]{2,1,0:T(8,128)S(1)}, u32[]{:S(2)}, u32[]{:S(2)}) collective-permute-start(f32[2,160,384]{2,1,0:T(8,128)} %copy-done.19), channel_id=1, source_target_pairs={{0,2},{1,3},{2,0},{3,1},{4,6},{5,7},{6,4},{7,5},{8,10},{9,11},{10,... | collective-permute-start | bytes 1474568 | tf_op jit(solution)/shard_map/ppermute | solution.py:322
  302.3 64.9 %collective-permute-start.5 = (f32[2,160,384]{2,1,0:T(8,128)}, f32[2,160,384]{2,1,0:T(8,128)S(1)}, u32[]{:S(2)}, u32[]{:S(2)}) collective-permute-start(f32[2,160,384]{2,1,0:T(8,128)} %copy-done.18), channel_id=1, source_target_pairs={{0,3},{1,0},{2,1},{3,2},{4,7},{5,4},{6,5},{7,6},{8,11},{9,8},{10,9... | collective-permute-start | bytes 1474568 | tf_op jit(solution)/shard_map/ppermute | solution.py:322
  303.7 92.4 %collective-permute-start = (f32[2,160,384]{2,1,0:T(8,128)}, f32[2,160,384]{2,1,0:T(8,128)S(1)}, u32[]{:S(2)}, u32[]{:S(2)}) collective-permute-start(f32[2,160,384]{2,1,0:T(8,128)} %copy-done.17), channel_id=1, source_target_pairs={{0,1},{1,2},{2,3},{3,0},{4,5},{5,6},{6,7},{7,4},{8,9},{9,10},{10,1... | collective-permute-start | bytes 1474568 | tf_op jit(solution)/shard_map/ppermute | solution.py:322
  303.7 102.9 %collective-permute-start.1 = (f32[2,160,384]{2,1,0:T(8,128)}, f32[2,160,384]{2,1,0:T(8,128)S(1)}, u32[]{:S(2)}, u32[]{:S(2)}) collective-permute-start(f32[2,160,384]{2,1,0:T(8,128)} %copy-done.16), channel_id=1, source_target_pairs={{0,2},{1,3},{2,0},{3,1},{4,6},{5,7},{6,4},{7,5},{8,10},{9,11},{10,... | collective-permute-start | bytes 1474568 | tf_op jit(solution)/shard_map/ppermute | solution.py:322
  319.0 100.5 %collective-permute-start.2 = (f32[2,160,384]{2,1,0:T(8,128)}, f32[2,160,384]{2,1,0:T(8,128)}, u32[]{:S(2)}, u32[]{:S(2)}) collective-permute-start(f32[2,160,384]{2,1,0:T(8,128)} %get-tuple-element.37), channel_id=1, source_target_pairs={{0,3},{1,0},{2,1},{3,2},{4,7},{5,4},{6,5},{7,6},{8,11},{9,8},{10,9... | collective-permute-start | bytes 1474568 | tf_op jit(solution)/shard_map/ppermute | solution.py:322
  344.2 78.3 %collective-permute-start.10 = (f32[2,160,384]{2,1,0:T(8,128)}, f32[2,160,384]{2,1,0:T(8,128)}, u32[]{:S(2)}, u32[]{:S(2)}) collective-permute-start(f32[2,160,384]{2,1,0:T(8,128)} %get-tuple-element.53), channel_id=1, source_target_pairs={{0,2},{1,3},{2,0},{3,1},{4,6},{5,7},{6,4},{7,5},{8,10},{9,11},{10,... | collective-permute-start | bytes 1474568 | tf_op jit(solution)/shard_map/ppermute | solution.py:322
  367.9 83.3 %collective-permute-start.11 = (f32[2,160,384]{2,1,0:T(8,128)}, f32[2,160,384]{2,1,0:T(8,128)}, u32[]{:S(2)}, u32[]{:S(2)}) collective-permute-start(f32[2,160,384]{2,1,0:T(8,128)} %get-tuple-element.54), channel_id=1, source_target_pairs={{0,3},{1,0},{2,1},{3,2},{4,7},{5,4},{6,5},{7,6},{8,11},{9,8},{10,9... | collective-permute-start | bytes 1474568 | tf_op jit(solution)/shard_map/ppermute | solution.py:322
  396.8 54.4 %collective-permute-start.9 = (f32[2,160,384]{2,1,0:T(8,128)}, f32[2,160,384]{2,1,0:T(8,128)}, u32[]{:S(2)}, u32[]{:S(2)}) collective-permute-start(f32[2,160,384]{2,1,0:T(8,128)} %get-tuple-element.52), channel_id=1, source_target_pairs={{0,1},{1,2},{2,3},{3,0},{4,5},{5,6},{6,7},{7,4},{8,9},{9,10},{10,1... | collective-permute-start | bytes 1474568 | tf_op jit(solution)/shard_map/ppermute | solution.py:322
  407.4 51.9 %collective-permute-start.6 = (f32[2,160,384]{2,1,0:T(8,128)}, f32[2,160,384]{2,1,0:T(8,128)}, u32[]{:S(2)}, u32[]{:S(2)}) collective-permute-start(f32[2,160,384]{2,1,0:T(8,128)} %get-tuple-element.46), channel_id=1, source_target_pairs={{0,1},{1,2},{2,3},{3,0},{4,5},{5,6},{6,7},{7,4},{8,9},{9,10},{10,1... | collective-permute-start | bytes 1474568 | tf_op jit(solution)/shard_map/ppermute | solution.py:322
  408.2 1.5 copy-start.5
  409.7 49.9 %copy-start.32 = (s32[4]{0:T(128)S(1)}, s32[4]{0:T(128)}, u32[]{:S(2)}) copy-start(s32[4]{0:T(128)} %get-tuple-element.85) | copy-start | bytes 52
  419.5 53.8 %copy-start.31 = (f32[384]{0:T(512)S(1)}, f32[384]{0:T(512)}, u32[]{:S(2)}) copy-start(f32[384]{0:T(512)} %param.14) | copy-start | bytes 4612
  419.5 71.3 %collective-permute-start.7 = (f32[2,160,384]{2,1,0:T(8,128)S(1)}, f32[2,160,384]{2,1,0:T(8,128)}, u32[]{:S(2)}, u32[]{:S(2)}) collective-permute-start(f32[2,160,384]{2,1,0:T(8,128)S(1)} %get-tuple-element.47), channel_id=1, source_target_pairs={{0,2},{1,3},{2,0},{3,1},{4,6},{5,7},{6,4},{7,5},{8,10},{9,11},{10,... | collective-permute-start | bytes 1474568 | tf_op jit(solution)/shard_map/ppermute | solution.py:322
  422.5 71.0 %collective-permute-start.8 = (f32[2,160,384]{2,1,0:T(8,128)S(1)}, f32[2,160,384]{2,1,0:T(8,128)}, u32[]{:S(2)}, u32[]{:S(2)}) collective-permute-start(f32[2,160,384]{2,1,0:T(8,128)S(1)} %get-tuple-element.48), channel_id=1, source_target_pairs={{0,3},{1,0},{2,1},{3,2},{4,7},{5,4},{6,5},{7,6},{8,11},{9,8},{10,9... | collective-permute-start | bytes 1474568 | tf_op jit(solution)/shard_map/ppermute | solution.py:322
  451.3 50.2 %collective-permute-start.12 = (f32[2,160,384]{2,1,0:T(8,128)}, f32[2,160,384]{2,1,0:T(8,128)}, u32[]{:S(2)}, u32[]{:S(2)}) collective-permute-start(f32[2,160,384]{2,1,0:T(8,128)} %get-tuple-element.58), channel_id=1, source_target_pairs={{0,1},{1,2},{2,3},{3,0},{4,5},{5,6},{6,7},{7,4},{8,9},{9,10},{10,1... | collective-permute-start | bytes 1474568 | tf_op jit(solution)/shard_map/ppermute | solution.py:322
  451.3 60.7 %collective-permute-start.13 = (f32[2,160,384]{2,1,0:T(8,128)}, f32[2,160,384]{2,1,0:T(8,128)}, u32[]{:S(2)}, u32[]{:S(2)}) collective-permute-start(f32[2,160,384]{2,1,0:T(8,128)} %get-tuple-element.59), channel_id=1, source_target_pairs={{0,2},{1,3},{2,0},{3,1},{4,6},{5,7},{6,4},{7,5},{8,10},{9,11},{10,... | collective-permute-start | bytes 1474568 | tf_op jit(solution)/shard_map/ppermute | solution.py:322
  459.3 55.2 %collective-permute-start.14 = (f32[2,160,384]{2,1,0:T(8,128)}, f32[2,160,384]{2,1,0:T(8,128)}, u32[]{:S(2)}, u32[]{:S(2)}) collective-permute-start(f32[2,160,384]{2,1,0:T(8,128)} %get-tuple-element.60), channel_id=1, source_target_pairs={{0,3},{1,0},{2,1},{3,2},{4,7},{5,4},{6,5},{7,6},{8,11},{9,8},{10,9... | collective-permute-start | bytes 1474568 | tf_op jit(solution)/shard_map/ppermute | solution.py:322
  468.5 50.3 %copy-start.7 = (f32[2,160,384]{2,1,0:T(8,128)S(1)}, f32[2,160,384]{2,1,0:T(8,128)}, u32[]{:S(2)}) copy-start(f32[2,160,384]{2,1,0:T(8,128)} %copy-done.6) | copy-start | bytes 1474564
  468.5 50.3 %copy-start.9 = (f32[2,160,384]{2,1,0:T(8,128)S(1)}, f32[2,160,384]{2,1,0:T(8,128)}, u32[]{:S(2)}) copy-start(f32[2,160,384]{2,1,0:T(8,128)} %copy-done.8) | copy-start | bytes 1474564
  468.5 50.3 %copy-start.22 = (f32[2,160,384]{2,1,0:T(8,128)S(1)}, f32[2,160,384]{2,1,0:T(8,128)}, u32[]{:S(2)}) copy-start(f32[2,160,384]{2,1,0:T(8,128)} %copy-done.21) | copy-start | bytes 1474564
  468.5 50.3 %copy-start.24 = (f32[2,160,384]{2,1,0:T(8,128)S(1)}, f32[2,160,384]{2,1,0:T(8,128)}, u32[]{:S(2)}) copy-start(f32[2,160,384]{2,1,0:T(8,128)} %copy-done.23) | copy-start | bytes 1474564
  473.3 45.5 %copy-start.26 = (f32[2,160,384]{2,1,0:T(8,128)S(1)}, f32[2,160,384]{2,1,0:T(8,128)}, u32[]{:S(2)}) copy-start(f32[2,160,384]{2,1,0:T(8,128)} %copy-done.25) | copy-start | bytes 1474564
  (20 other events, 18.8 us)
